TPU v7x, 128 devices: a whole 4x4x4 slice. The times are simulated.
128 devices in a mesh: dp: 8 (over z, x_hi), seq: 16 (over y, x_lo, core).
Axes of the slice: x: 4 (x_hi: 2, x_lo: 2; x = x_hi * 2 + x_lo), y: 4, z: 4, core: 2. Of those that a mesh axis runs over, the one named last changes fastest.
Arguments:
- layer_input: bfloat16 [8, 64, 256, 1152], P('dp', 'seq'), may hold values from -8 to 8
- queries: bfloat16 [8, 64, 256, 1152], P('dp', 'seq'), may hold values from -5 to 5
- keys: bfloat16 [8, 64, 256, 1152], P('dp', 'seq'), may hold values from -5 to 5
- values: bfloat16 [8, 64, 256, 1152], P('dp', 'seq'), may hold values from -6 to 6
- d_attn: bfloat16 [8, 64, 256, 1152], P('dp', 'seq'), may hold values from -6 to 6
- w_qkv: bfloat16 [1152, 3456], replicated, may hold values from -0.1875 to 0.1875
Outputs:
- d_input: bfloat16 [8, 64, 256, 1152], P('dp', 'seq')
- d_weight: float32 [1152, 3456], P('seq')
All inputs are finite; a program needn't handle non-finite values.
Results may differ from a plain program's by a relative error of at most 0.0068.
Values may be sent and summed in bfloat16 or wider, within the bound.
No kernel may reach another device: no remote copies, remote signals or barrier semaphores. Data moves between devices by JAX's collectives and lax.ppermute only.
A program may use at most 192 MiB of HBM per device.

v0:
```python
import functools
import math

import jax
import jax.numpy as jnp
from jax import lax
from jax.experimental import pallas as pl
from jax.experimental.pallas import tpu as pltpu
from jax.sharding import Mesh
from jax.sharding import PartitionSpec as P

HEADS = 16
HEAD_DIM = 72
FRAMES = 64
SPATIAL = 256
WIDTH = HEADS * HEAD_DIM
LANES = 128
TILES = WIDTH // LANES
FACTOR = HEAD_DIM ** (-0.5)
SEQ = ("y", "xl", "core")
EARLY_ROWS = 256
SPLIT = 1792
MIB = 1024 * 1024


def pack_kernel(cells, group, *refs):
    out_ref = refs[-1]
    for n, ref in enumerate(refs[:-1]):
        for i in range(group):
            out_ref[i, n] = ref[0, :, i * cells : (i + 1) * cells, :]


def pack(arrays, devices):
    frames, cells = arrays[0].shape[1], arrays[0].shape[2] // devices
    group = 4
    block = pl.BlockSpec((1, frames, group * cells, WIDTH), lambda j: (0, 0, j, 0))
    count = len(arrays)
    return pl.pallas_call(
        functools.partial(pack_kernel, cells, group),
        grid=(devices // group,),
        in_specs=[block] * count,
        out_specs=pl.BlockSpec((group, count, frames, cells, WIDTH), lambda j: (j, 0, 0, 0, 0)),
        out_shape=jax.ShapeDtypeStruct((devices, count, frames, cells, WIDTH), jnp.bfloat16),
        compiler_params=pltpu.CompilerParams(vmem_limit_bytes=60 * MIB),
        cost_estimate=pl.CostEstimate(
            flops=0, bytes_accessed=2 * count * arrays[0].size * 2, transcendentals=0
        ),
    )(*arrays)


def unpack_kernel(cells, group, in_ref, out_ref):
    for i in range(group):
        out_ref[0, :, i * cells : (i + 1) * cells, :] = in_ref[i]


def unpack(blocks):
    devices, frames, cells, width = blocks.shape
    group = 4
    return pl.pallas_call(
        functools.partial(unpack_kernel, cells, group),
        grid=(devices // group,),
        in_specs=[pl.BlockSpec((group, frames, cells, width), lambda j: (j, 0, 0, 0))],
        out_specs=pl.BlockSpec((1, frames, group * cells, width), lambda j: (0, 0, j, 0)),
        out_shape=jax.ShapeDtypeStruct((1, frames, cells * devices, width), jnp.bfloat16),
        compiler_params=pltpu.CompilerParams(vmem_limit_bytes=60 * MIB),
        cost_estimate=pl.CostEstimate(flops=0, bytes_accessed=4 * blocks.size, transcendentals=0),
    )(blocks)


def dot_nt(a, b):
    return lax.dot_general(a, b, (((1,), (1,)), ((), ())), preferred_element_type=jnp.float32)


def dot_tn(a, b):
    return lax.dot_general(a, b, (((0,), (0,)), ((), ())), preferred_element_type=jnp.float32)


def dot_nn(a, b):
    return jnp.dot(a, b, preferred_element_type=jnp.float32)


def attend_kernel(
    cells, r_ref, w_hbm, g0_ref, g1_ref, i_hbm, q_scr, k_scr, v_scr, d_scr, w_scr, i_scr, w_sem, i_sem
):
    w_copy = pltpu.make_async_copy(w_hbm, w_scr, w_sem)
    w_copy.start()
    rows = FRAMES * cells
    scratches = (q_scr, k_scr, v_scr, d_scr)
    for n, scr in enumerate(scratches):
        for t in range(TILES):
            tile = r_ref[:, n, :, :, t * LANES : (t + 1) * LANES]
            scr[t] = tile.reshape(rows, LANES).astype(jnp.float32)

    pair_rows = 2 * FRAMES
    lane = lax.broadcasted_iota(jnp.int32, (FRAMES, 2 * pair_rows), 1)
    left = lane % pair_rows < FRAMES

    def compact(block):
        return jnp.where(left, block[:FRAMES], block[FRAMES:])

    def spread(block):
        zero = jnp.zeros_like(block)
        upper = jnp.where(left, block, zero)
        lower = jnp.where(left, zero, block)
        return jnp.concatenate([upper, lower], axis=0).astype(jnp.bfloat16)

    def pair_step(i, carry):
        p = 2 * i

        def load(scr, t):
            first = scr[t, pl.ds(p, FRAMES, stride=cells), :]
            second = scr[t, pl.ds(p + 1, FRAMES, stride=cells), :]
            return jnp.concatenate([first, second], axis=0).astype(jnp.bfloat16)

        q_t, k_t, v_t, d_t = ([load(scr, t) for t in range(TILES)] for scr in scratches)
        acc = [dict(), dict(), dict()]

        def put(n, t, value):
            acc[n][t] = acc[n][t] + value if t in acc[n] else value

        def scores(h):
            start = h * HEAD_DIM
            first = start // LANES
            low = start - first * LANES
            window_lane = lax.broadcasted_iota(jnp.int32, (1, 2 * LANES), 1)
            masks = [
                ((window_lane >= lo) & (window_lane < lo + HEAD_DIM)).astype(jnp.bfloat16)
                for lo in (low, low + HEAD_DIM)
            ]

            def window(parts):
                return jnp.concatenate([parts[first], parts[first + 1]], axis=1)

            def both(value):
                return jnp.concatenate([value * mask for mask in masks], axis=0)

            k_w = window(k_t)
            q_h = both(window(q_t))
            d_h = both(window(d_t))
            raw = compact(dot_nt(k_w, q_h))
            grad_p = compact(dot_nt(window(v_t), d_h))
            return k_w, q_h, d_h, raw, grad_p

        def soft(k_w, q_h, d_h, raw, grad_p):
            exp_term = jnp.exp((raw - jnp.max(raw, axis=0, keepdims=True)) * FACTOR)
            prob = exp_term * (1.0 / jnp.sum(exp_term, axis=0, keepdims=True))
            prob_low = prob.astype(jnp.bfloat16).astype(jnp.float32)
            delta = jnp.sum(prob_low * grad_p, axis=0, keepdims=True)
            grad_s = spread(prob * (grad_p - delta))
            return k_w, q_h, d_h, spread(prob), grad_s

        def grads(h, k_w, q_h, d_h, prob_low, grad_s):
            start = h * HEAD_DIM
            first = start // LANES
            low = start - first * LANES
            window_lane = lax.broadcasted_iota(jnp.int32, (1, 2 * LANES), 1)
            own = (window_lane >= low) & (window_lane < low + 2 * HEAD_DIM)
            from_keys = dot_tn(grad_s, k_w)
            halves = jnp.where(
                window_lane < low + HEAD_DIM, from_keys[:pair_rows], from_keys[pair_rows:]
            )
            results = (
                jnp.where(own, halves, 0.0),
                dot_nn(grad_s, q_h),
                dot_nn(prob_low, d_h),
            )
            for n, result in enumerate(results):
                put(n, first, result[:, :LANES])
                put(n, first + 1, result[:, LANES:])
            for t in range(first, (start + 2 * HEAD_DIM) // LANES):
                for n, scr in enumerate((q_scr, k_scr, v_scr)):
                    value = acc[n].pop(t)
                    scr[t, pl.ds(p, FRAMES, stride=cells), :] = value[:FRAMES]
                    scr[t, pl.ds(p + 1, FRAMES, stride=cells), :] = value[FRAMES:]

        steps = HEADS // 2
        scored, softened = {}, {}
        for at in range(steps + 2):
            if at < steps:
                scored[at] = scores(2 * at)
            if at >= 2:
                grads(2 * (at - 2), *softened.pop(at - 2))
            if 1 <= at <= steps:
                softened[at - 1] = soft(*scored.pop(at - 1))
        return carry

    lax.fori_loop(0, cells // 2, pair_step, 0)
    for n, scr in enumerate((q_scr, k_scr, v_scr)):
        for t in range(TILES):
            lo = n * WIDTH + t * LANES
            scale = 1.0 if n == 2 else FACTOR
            g_ref, lo = (g0_ref, lo) if lo < SPLIT else (g1_ref, lo - SPLIT)
            g_ref[:, lo : lo + LANES] = (scr[t] * scale).astype(jnp.bfloat16)
    w_copy.wait()
    i_scr[...] = (
        dot_nt(g0_ref[:EARLY_ROWS, :], w_scr[:, :SPLIT])
        + dot_nt(g1_ref[:EARLY_ROWS, :], w_scr[:, SPLIT:])
    ).astype(jnp.bfloat16)
    i_copy = pltpu.make_async_copy(i_scr, i_hbm.at[pl.ds(0, EARLY_ROWS), :], i_sem)
    i_copy.start()
    i_copy.wait()


def attend(received, weight):
    devices, _, frames, cells, _ = received.shape
    rows = devices * frames * cells
    scratch = pltpu.VMEM((TILES, rows, LANES), jnp.float32)
    vmem = pl.BlockSpec(memory_space=pltpu.VMEM)
    return pl.pallas_call(
        functools.partial(attend_kernel, cells),
        in_specs=[vmem, pl.BlockSpec(memory_space=pl.ANY)],
        out_specs=[vmem, vmem, pl.BlockSpec(memory_space=pltpu.HBM)],
        out_shape=[
            jax.ShapeDtypeStruct((rows, SPLIT), jnp.bfloat16),
            jax.ShapeDtypeStruct((rows, 3 * WIDTH - SPLIT), jnp.bfloat16),
            jax.ShapeDtypeStruct((rows, WIDTH), jnp.bfloat16),
        ],
        scratch_shapes=[scratch] * 4
        + [
            pltpu.VMEM(weight.shape, jnp.bfloat16),
            pltpu.VMEM((EARLY_ROWS, WIDTH), jnp.bfloat16),
            pltpu.SemaphoreType.DMA,
            pltpu.SemaphoreType.DMA,
        ],
        compiler_params=pltpu.CompilerParams(vmem_limit_bytes=60 * MIB),
        cost_estimate=pl.CostEstimate(
            flops=24_000_000_000, bytes_accessed=14 * rows * WIDTH, transcendentals=4_000_000
        ),
    )(received, weight)


def input_grad_kernel(g0_ref, g1_ref, w_ref, early_ref, after_ref, out_ref):
    out_ref[...] = (
        dot_nt(g0_ref[...], w_ref[:, :SPLIT]) + dot_nt(g1_ref[...], w_ref[:, SPLIT:])
    ).astype(jnp.bfloat16)


def input_grad(grads, weight, early, after):
    rows, depth = early.shape[0], weight.shape[1]
    step = EARLY_ROWS
    return pl.pallas_call(
        input_grad_kernel,
        grid=(rows // step - 1,),
        in_specs=[
            pl.BlockSpec((step, SPLIT), lambda j: (j + 1, 0)),
            pl.BlockSpec((step, depth - SPLIT), lambda j: (j + 1, 0)),
            pl.BlockSpec((WIDTH, depth), lambda j: (0, 0)),
            pl.BlockSpec(memory_space=pl.ANY),
            pl.BlockSpec(memory_space=pl.ANY),
        ],
        out_specs=pl.BlockSpec((step, WIDTH), lambda j: (j + 1, 0)),
        out_shape=jax.ShapeDtypeStruct((rows, WIDTH), jnp.bfloat16),
        input_output_aliases={3: 0},
        compiler_params=pltpu.CompilerParams(vmem_limit_bytes=60 * MIB),
        cost_estimate=pl.CostEstimate(
            flops=2 * rows * depth * WIDTH,
            bytes_accessed=2 * depth * (rows + WIDTH),
            transcendentals=0,
        ),
    )(*grads, weight, early, after)


def multiply(turned, g_ref, out_ref, first):
    owners, share, step = out_ref.shape[1:]
    wide = dot_nn(turned, g_ref[...])
    width = wide.shape[1]
    for n in range(-(-width // step)):
        end = min(step, width - n * step)
        for block in range(owners):
            piece = wide[block * share : (block + 1) * share, n * step : n * step + end]
            out_ref[first + n, block, :, :end] = piece.astype(jnp.bfloat16)
        if end < step:
            out_ref[first + n, :, :, end:] = jnp.zeros((owners, share, step - end), jnp.bfloat16)


def turn_kernel(core_ref, x_hbm, g_ref, out_ref, own_ref, sent_ref, x_scr, wide_scr, x_sems):
    chunks, rows = x_scr.shape[:2]
    share = out_ref.shape[2]
    x_copies = [
        pltpu.make_async_copy(x_hbm.at[pl.ds(i * rows, rows), :], x_scr.at[i], x_sems.at[i])
        for i in range(chunks)
    ]
    for copy in x_copies:
        copy.start()
    for i, copy in enumerate(x_copies):
        copy.wait()
        flipped = x_scr[i].astype(jnp.float32).T
        for n, turned_ref in enumerate((own_ref, sent_ref)):
            for block in range(out_ref.shape[1]):
                lo = 2 * block * share
                even, odd = flipped[lo : lo + share], flipped[lo + share : lo + 2 * share]
                wide_scr[n, block * share : (block + 1) * share, :] = jnp.where(
                    core_ref[0] == n, even, odd
                )
            turned_ref[:, i * rows : (i + 1) * rows] = wide_scr[n].astype(jnp.bfloat16)
    multiply(sent_ref[...], g_ref, out_ref, 0)


def product_kernel(turned_ref, *refs):
    out_ref = refs[-1]
    first = 0
    for g_ref in refs[:-1]:
        multiply(turned_ref[...], g_ref, out_ref, first)
        first += g_ref.shape[1] // out_ref.shape[3]


def turn_and_product(core, tokens, grads, parts, step, owners):
    rows, chunks = tokens.shape[0], 4
    half = WIDTH // 2
    vmem = pl.BlockSpec(memory_space=pltpu.VMEM)
    hbm = pl.BlockSpec(memory_space=pltpu.HBM)
    turned = jax.ShapeDtypeStruct((half, rows), jnp.bfloat16)
    return pl.pallas_call(
        turn_kernel,
        in_specs=[pl.BlockSpec(memory_space=pltpu.SMEM), hbm, vmem],
        out_specs=[vmem, vmem, vmem],
        out_shape=[
            jax.ShapeDtypeStruct((parts, owners, half // owners, step), jnp.bfloat16),
            turned,
            turned,
        ],
        scratch_shapes=[
            pltpu.VMEM((chunks, rows // chunks, WIDTH), jnp.bfloat16),
            pltpu.VMEM((2, half, rows // chunks), jnp.float32),
            pltpu.SemaphoreType.DMA((chunks,)),
        ],
        compiler_params=pltpu.CompilerParams(vmem_limit_bytes=36 * MIB),
        cost_estimate=pl.CostEstimate(
            flops=rows * WIDTH * step * parts,
            bytes_accessed=rows * (2 * WIDTH + 2 * step * parts) + WIDTH * step * parts,
            transcendentals=0,
        ),
    )(core, tokens, grads)


def product(turned, ranges, parts, step, owners):
    half, rows = turned.shape
    vmem = pl.BlockSpec(memory_space=pltpu.VMEM)
    return pl.pallas_call(
        product_kernel,
        in_specs=[vmem] * (1 + len(ranges)),
        out_specs=vmem,
        out_shape=jax.ShapeDtypeStruct((parts, owners, half // owners, step), jnp.bfloat16),
        compiler_params=pltpu.CompilerParams(vmem_limit_bytes=36 * MIB),
        cost_estimate=pl.CostEstimate(
            flops=rows * WIDTH * step * parts,
            bytes_accessed=rows * (WIDTH + 2 * step * parts) + WIDTH * step * parts,
            transcendentals=0,
        ),
    )(turned, *ranges)


def add_kernel(own_ref, early_ref, late_ref, out_ref):
    half = pl.num_programs(0) // 2
    at = pl.program_id(0)

    @pl.when(at < half)
    def _():
        out_ref[...] = add(own_ref[...], early_ref[...])

    @pl.when(at >= half)
    def _():
        out_ref[...] = add(own_ref[...], late_ref[...])


def add_parts(own, early, late):
    parts = own.shape[0]
    half = parts // 2
    block = (1,) + own.shape[1:]
    return pl.pallas_call(
        add_kernel,
        grid=(parts,),
        in_specs=[
            pl.BlockSpec(block, lambda j: (j, 0, 0, 0)),
            pl.BlockSpec(block, lambda j: (jnp.minimum(j, half - 1), 0, 0, 0)),
            pl.BlockSpec(block, lambda j: (jnp.maximum(j - half, 0), 0, 0, 0)),
        ],
        out_specs=pl.BlockSpec(block, lambda j: (j, 0, 0, 0)),
        out_shape=jax.ShapeDtypeStruct(own.shape, own.dtype),
        compiler_params=pltpu.CompilerParams(vmem_limit_bytes=36 * MIB),
        cost_estimate=pl.CostEstimate(
            flops=own.size, bytes_accessed=6 * own.size, transcendentals=0
        ),
    )(own, early, late)


def swap(value, axis):
    return lax.ppermute(value, axis, [(0, 1), (1, 0)])


def add(first, second):
    return (first.astype(jnp.float32) + second.astype(jnp.float32)).astype(jnp.bfloat16)


def fold_kernel(blocks_ref, after_ref, out_ref):
    total = blocks_ref[0].astype(jnp.float32)
    for n in range(1, blocks_ref.shape[0]):
        total = total + blocks_ref[n].astype(jnp.float32)
    out_ref[...] = total.astype(jnp.bfloat16)


def fold(blocks, after):
    vmem = pl.BlockSpec(memory_space=pltpu.VMEM)
    return pl.pallas_call(
        fold_kernel,
        in_specs=[vmem, pl.BlockSpec(memory_space=pl.ANY)],
        out_specs=vmem,
        out_shape=jax.ShapeDtypeStruct(blocks.shape[1:], jnp.bfloat16),
        compiler_params=pltpu.CompilerParams(vmem_limit_bytes=16 * MIB),
        cost_estimate=pl.CostEstimate(
            flops=blocks.size, bytes_accessed=2 * blocks.size, transcendentals=0
        ),
    )(blocks, after)


def join_kernel(scale, z_ref, *refs):
    out_ref = refs[-1]
    parts = len(refs) - 1
    step = refs[0].shape[1]
    whole = out_ref.shape[1] - (parts - 1) * step
    for n, ref in enumerate(refs[:-1]):
        part = z_ref[0] ^ n
        lo = pl.multiple_of(part * step, LANES)
        out_ref[:, pl.ds(lo, whole)] = ref[:, :whole].astype(jnp.float32) * scale

        @pl.when(part < parts - 1)
        def _():
            rest = pl.multiple_of(part * step + whole, LANES)
            out_ref[:, pl.ds(rest, step - whole)] = ref[:, whole:].astype(jnp.float32) * scale


def join(z, blocks, scale):
    vmem = pl.BlockSpec(memory_space=pltpu.VMEM)
    rows = blocks[0].shape[0]
    return pl.pallas_call(
        functools.partial(join_kernel, scale),
        in_specs=[pl.BlockSpec(memory_space=pltpu.SMEM)] + [vmem] * len(blocks),
        out_specs=vmem,
        out_shape=jax.ShapeDtypeStruct((rows, 3 * WIDTH), jnp.float32),
        compiler_params=pltpu.CompilerParams(vmem_limit_bytes=16 * MIB),
        cost_estimate=pl.CostEstimate(
            flops=rows * 3 * WIDTH, bytes_accessed=6 * rows * 3 * WIDTH, transcendentals=0
        ),
    )(z, *blocks)


def per_device(layer_input, queries, keys, values, d_attn, w_qkv):
    devices = lax.axis_size(SEQ)
    parts = lax.axis_size("z")
    owners = devices // lax.axis_size("core")
    clips = parts * lax.axis_size("xh")
    frames, spatial = layer_input.shape[1], layer_input.shape[2]
    cells = spatial // devices
    rows = devices * frames * cells
    norm_scale = 1.0 / math.sqrt(clips * FRAMES * SPATIAL)
    core = lax.axis_index("core").reshape(1).astype(jnp.int32)

    sent = pack([queries, keys, values, d_attn], devices)
    received = lax.all_to_all(sent, SEQ, 0, 0, tiled=True)
    sent_x = pack([layer_input], devices)
    tokens = lax.all_to_all(sent_x, SEQ, 0, 0, tiled=True).reshape(rows, WIDTH)

    *grads, early = attend(received, w_qkv)
    step = -(-3 * WIDTH // (parts * LANES)) * LANES
    count = parts // 2
    sent_early, turned_own, turned_sent = turn_and_product(
        core, tokens, grads[0], count, step, owners
    )
    sent_late = product(turned_sent, grads[1:], count, step, owners)
    got_early, got_late = swap(sent_early, "core"), swap(sent_late, "core")
    own_part = product(turned_own, grads, parts, step, owners)
    kept = add_parts(own_part, got_early, got_late)
    over_z = lax.psum_scatter(kept, "z", scatter_dimension=0, tiled=True)[0]

    d_local = input_grad(grads, w_qkv, early, kept).reshape(devices, frames, cells, WIDTH)
    d_input = unpack(lax.all_to_all(d_local, SEQ, 0, 0, tiled=True))

    share = fold(lax.all_to_all(over_z, ("y", "xl"), 0, 0, tiled=True), d_input)
    share = add(share, swap(share, "xh"))
    blocks = [share] + [
        lax.ppermute(share, "z", [(i, i ^ n) for i in range(parts)]) for n in range(1, parts)
    ]
    d_weight = join(lax.axis_index("z").reshape(1).astype(jnp.int32), blocks, norm_scale)
    return (d_input, d_weight)


def solution(mesh):
    sizes = (4, 2, 4, 2, 2)
    fine = Mesh(mesh.devices.reshape(sizes), ("z", "xh", "y", "xl", "core"))
    dp = ("z", "xh")
    block = P(dp, SEQ, None, None)
    return jax.shard_map(
        per_device,
        mesh=fine,
        in_specs=(block,) * 5 + (P(),),
        out_specs=(block, P(SEQ, None)),
        check_vma=False,
    )
```

profile of v0, /device:TPU:0, one launch (start us, length us, event | category | flops | bytes accessed | tf_op | source)
XLA Modules:
  0.0 273.8 jit_solution(17319607090942115859)
XLA Ops:
  7.2 7.5 %shard_map.77 = bf16[16,4,4,16,1152]{4,3,2,1,0:T(8,128)(2,1)} custom-call(bf16[1,4,256,1152]{3,2,1,0:T(8,128)(2,1)} %refs_0_.2, bf16[1,4,256,1152]{3,2,1,0:T(8,128)(2,1)} %refs_1_.1, bf16[1,4,256,1152]{3,2,1,0:T(8,128)(2,1)} %refs_2_.1, bf16[1,4,256,1152]{3,2,1,0:T(8,128)(2,1)} %refs_3_.1), custom_call_target="tpu_custom_call" | custom-call | bytes 18874368 | tf_op jit(solution)/shard_map/pallas_call | solution.py:38
  14.7 5.6 %all-to-all-start = ((bf16[16,4,4,16,1152]{4,3,2,1,0:T(8,128)(2,1)}), bf16[16,4,4,16,1152]{4,3,2,1,0:T(8,128)(2,1)}, u32[]{:S(2)}, u32[]{:S(2)}) async-start(bf16[16,4,4,16,1152]{4,3,2,1,0:T(8,128)(2,1)} %shard_map.77), calls=%async_computation | async-start | bytes 18874368 | tf_op jit(solution)/shard_map/all_to_all | solution.py:459
  20.4 3.9 %shard_map.79 = bf16[16,1,4,16,1152]{4,3,2,1,0:T(8,128)(2,1)} custom-call(bf16[1,4,256,1152]{3,2,1,0:T(8,128)(2,1)} %refs_0_.3), custom_call_target="tpu_custom_call" | custom-call | bytes 4718592 | tf_op jit(solution)/shard_map/pallas_call | solution.py:38
  24.2 102.7 %all-to-all-done.r_ref = bf16[16,4,4,16,1152]{4,3,2,1,0:T(8,128)(2,1)} async-done(((bf16[16,4,4,16,1152]{4,3,2,1,0:T(8,128)(2,1)}), bf16[16,4,4,16,1152]{4,3,2,1,0:T(8,128)(2,1)}, u32[]{:S(2)}, u32[]{:S(2)}) %all-to-all-start) | async-done | bytes 9437216 | tf_op jit(solution)/shard_map/all_to_all | solution.py:459
  126.9 3.7 %all-to-all-start.1 = ((bf16[16,1,4,16,1152]{4,3,2,1,0:T(8,128)(2,1)}), bf16[16,1,4,16,1152]{4,3,2,1,0:T(8,128)(2,1)S(1)}, u32[]{:S(2)}, u32[]{:S(2)}) async-start(bf16[16,1,4,16,1152]{4,3,2,1,0:T(8,128)(2,1)} %shard_map.79), calls=%async_computation.1 | async-start | bytes 4718592 | tf_op jit(solution)/shard_map/all_to_all | solution.py:461
  130.7 0.0 reduce-scatter.2.cloned.1.call-start
  130.7 30.4 %shard_map.78 = (bf16[1024,1792]{1,0:T(8,128)(2,1)}, bf16[1024,1664]{1,0:T(8,128)(2,1)}, bf16[1024,1152]{1,0:T(8,128)(2,1)}) custom-call(bf16[16,4,4,16,1152]{4,3,2,1,0:T(8,128)(2,1)} %all-to-all-done.r_ref, bf16[1152,3456]{1,0:T(8,128)(2,1)} %w_ref.1), custom_call_target="tpu_custom_call" | custom-call | flops 24000000000 | bytes 16515072 | tf_op jit(solution)/shard_map/pallas_call | solution.py:209
  161.1 0.2 all-to-all-done.1
  161.3 0.0 copy-start.3
  161.3 2.0 copy-done.3
  163.4 0.0 copy-start.2
  163.4 3.6 %shard_map.80 = (bf16[2,8,72,896]{3,2,1,0:T(8,128)(2,1)S(1)}, bf16[576,1024]{1,0:T(8,128)(2,1)S(1)}, bf16[576,1024]{1,0:T(8,128)(2,1)S(1)}) custom-call(s32[1]{0:T(128)} %bitcast.core_ref, bf16[1024,1152]{1,0:T(8,128)(2,1)S(1)} %bitcast.5, bf16[1024,1792]{1,0:T(8,128)(2,1)S(1)} %copy-done.3), custom_call_target="tpu_custom_call" | custom-call | flops 2113929216 | bytes 8093696 | tf_op jit(solution)/shard_map/pallas_call | solution.py:313
  167.0 0.0 copy-done.2
  167.0 0.0 copy-start.4
  167.0 2.3 shard_map.82
  169.3 0.2 collective-permute-start.1
  169.5 0.4 collective-permute-start
  169.9 0.0 copy-done.4
  169.9 4.4 %shard_map.81.own_ref = bf16[4,8,72,896]{3,2,1,0:T(8,128)(2,1)S(1)} custom-call(bf16[576,1024]{1,0:T(8,128)(2,1)S(1)} %get-tuple-element.11.turned_ref, bf16[1024,1792]{1,0:T(8,128)(2,1)S(1)} %copy-done.4, bf16[1024,1664]{1,0:T(8,128)(2,1)S(1)} %copy-done.2), custom_call_target="tpu_custom_call" | custom-call | flops 4227858432 | bytes 12648448 | tf_op jit(solution)/shard_map/pallas_call | solution.py:339
  174.3 0.0 collective-permute-done.1.late_ref
  174.4 2.1 collective-permute-done.early_ref
  176.5 1.0 shard_map.83.after_ref
  177.5 0.0 copy-start
  177.5 1.9 copy-done
  179.4 0.0 reduce-scatter.2.cloned.1.call-update
  179.5 12.5 %shard_map.84 = bf16[1024,1152]{1,0:T(8,128)(2,1)} custom-call(bf16[1024,1792]{1,0:T(8,128)(2,1)} %get-tuple-element.8.g_ref.refs_0_.g0_ref, bf16[1024,1664]{1,0:T(8,128)(2,1)} %get-tuple-element.9.refs_1_.refs_0_.g1_ref, bf16[1152,3456]{1,0:T(8,128)(2,1)} %w_ref.1, bf16[1024,1152]{1,0:T(8,128)(2,1)} %get-tuple-element.10.early_ref, ...), custom_call_target="tpu_custom_call", output_to_operand_aliasing={{}: (3, {})} | custom-call | flops 8153726976 | bytes 15040512 | tf_op jit(solution)/shard_map/pallas_call | solution.py:241
  191.9 36.1 %all_to_all.20.in_ref = bf16[16,4,16,1152]{3,2,1,0:T(8,128)(2,1)} all-to-all(bf16[16,4,16,1152]{3,2,1,0:T(8,128)(2,1)} %bitcast.6), channel_id=1, replica_groups=mesh['z'=4,'xh'=2,'y'=4,'xl'=2,'core'=2] {'y','xl','core'}, dimensions={0} | all-to-all | bytes 4718592 | tf_op jit(solution)/shard_map/all_to_all | solution.py:476
  228.0 0.2 reduce-scatter.2.cloned.1.call-done
  228.2 5.2 %all-to-all-start.3 = ((bf16[8,72,896]{2,1,0:T(8,128)(2,1)}), bf16[8,72,896]{2,1,0:T(8,128)(2,1)S(1)}, u32[]{:S(2)}, u32[]{:S(2)}) async-start(bf16[8,72,896]{2,1,0:T(8,128)(2,1)} %bitcast.7), calls=%async_computation.4 | async-start | bytes 2064384 | tf_op jit(solution)/shard_map/all_to_all | solution.py:478
  233.4 3.9 %shard_map.85.after_ref = bf16[1,4,256,1152]{3,2,1,0:T(8,128)(2,1)} custom-call(bf16[16,4,16,1152]{3,2,1,0:T(8,128)(2,1)} %all_to_all.20.in_ref), custom_call_target="tpu_custom_call" | custom-call | bytes 4718592 | tf_op jit(solution)/shard_map/pallas_call | solution.py:59
  237.3 11.7 %all-to-all-done.3.blocks_ref = bf16[8,72,896]{2,1,0:T(8,128)(2,1)S(1)} async-done(((bf16[8,72,896]{2,1,0:T(8,128)(2,1)}), bf16[8,72,896]{2,1,0:T(8,128)(2,1)S(1)}, u32[]{:S(2)}, u32[]{:S(2)}) %all-to-all-start.3) | async-done | bytes 1032224 | tf_op jit(solution)/shard_map/all_to_all | solution.py:478
  248.9 0.0 copy-start.1
  248.9 1.7 copy-done.1
  250.6 0.1 shard_map.86
  250.7 2.8 %collective-permute-start.2 = (bf16[72,896]{1,0:T(8,128)(2,1)S(1)}, bf16[72,896]{1,0:T(8,128)(2,1)S(1)}, u32[]{:S(2)}, u32[]{:S(2)}) collective-permute-start(bf16[72,896]{1,0:T(8,128)(2,1)S(1)} %shard_map.86), channel_id=1, source_target_pairs={{0,16},{16,0},{1,17},{17,1},{2,18},{18,2},{3,19},{19,3},{4,20},{20... | collective-permute-start | bytes 387080 | tf_op jit(solution)/shard_map/ppermute | solution.py:388
  253.5 3.8 %collective-permute-done.2 = bf16[72,896]{1,0:T(8,128)(2,1)S(1)} collective-permute-done((bf16[72,896]{1,0:T(8,128)(2,1)S(1)}, bf16[72,896]{1,0:T(8,128)(2,1)S(1)}, u32[]{:S(2)}, u32[]{:S(2)}) %collective-permute-start.2) | collective-permute-done | bytes 129056 | tf_op jit(solution)/shard_map/ppermute | solution.py:388
  257.3 2.2 collective-permute-start.5
  259.5 0.1 collective-permute-start.4
  259.6 1.8 collective-permute-start.3
  261.5 2.1 collective-permute-done.5.refs_3_
  263.5 2.4 collective-permute-done.4.refs_2_
  265.9 0.0 collective-permute-done.3.refs_1_
  265.9 1.0 shard_map.87
  (1 shorter events, 0.0 us)
Async XLA Ops:
  14.7 112.2 %all-to-all-start = ((bf16[16,4,4,16,1152]{4,3,2,1,0:T(8,128)(2,1)}), bf16[16,4,4,16,1152]{4,3,2,1,0:T(8,128)(2,1)}, u32[]{:S(2)}, u32[]{:S(2)}) async-start(bf16[16,4,4,16,1152]{4,3,2,1,0:T(8,128)(2,1)} %shard_map.77), calls=%async_computation | async-start | bytes 18874368 | tf_op jit(solution)/shard_map/all_to_all | solution.py:459
  126.9 34.4 %all-to-all-start.1 = ((bf16[16,1,4,16,1152]{4,3,2,1,0:T(8,128)(2,1)}), bf16[16,1,4,16,1152]{4,3,2,1,0:T(8,128)(2,1)S(1)}, u32[]{:S(2)}, u32[]{:S(2)}) async-start(bf16[16,1,4,16,1152]{4,3,2,1,0:T(8,128)(2,1)} %shard_map.79), calls=%async_computation.1 | async-start | bytes 4718592 | tf_op jit(solution)/shard_map/all_to_all | solution.py:461
  130.7 97.5 %reduce-scatter.2.cloned.1.call-start = ((), (), s32[]{:S(2)}) async-start(), calls=%async_computation.5 | async-start | bytes 5160960 | tf_op jit(solution)/shard_map/reduce_scatter | solution.py:473
  161.3 2.0 copy-start.3
  163.4 3.6 %copy-start.2 = (bf16[1024,1664]{1,0:T(8,128)(2,1)S(1)}, bf16[1024,1664]{1,0:T(8,128)(2,1)}, u32[]{:S(2)}) copy-start(bf16[1024,1664]{1,0:T(8,128)(2,1)} %get-tuple-element.9.refs_1_.refs_0_.g1_ref) | copy-start | bytes 10223620
  167.0 2.9 %copy-start.4 = (bf16[1024,1792]{1,0:T(8,128)(2,1)S(1)}, bf16[1024,1792]{1,0:T(8,128)(2,1)}, u32[]{:S(2)}) copy-start(bf16[1024,1792]{1,0:T(8,128)(2,1)} %get-tuple-element.8.g_ref.refs_0_.g0_ref) | copy-start | bytes 11010052
  169.3 5.0 %collective-permute-start.1 = (bf16[2,8,72,896]{3,2,1,0:T(8,128)(2,1)S(1)}, bf16[2,8,72,896]{3,2,1,0:T(8,128)(2,1)S(1)}, u32[]{:S(2)}, u32[]{:S(2)}) collective-permute-start(bf16[2,8,72,896]{3,2,1,0:T(8,128)(2,1)S(1)} %shard_map.82), channel_id=1, source_target_pairs={{0,1},{1,0},{2,3},{3,2},{4,5},{5,4},{6,7},{7,6},{8,9},{9,8},{10,11... | collective-permute-start | bytes 6193160 | tf_op jit(solution)/shard_map/ppermute | solution.py:388
  169.5 7.0 %collective-permute-start = (bf16[2,8,72,896]{3,2,1,0:T(8,128)(2,1)S(1)}, bf16[2,8,72,896]{3,2,1,0:T(8,128)(2,1)S(1)}, u32[]{:S(2)}, u32[]{:S(2)}) collective-permute-start(bf16[2,8,72,896]{3,2,1,0:T(8,128)(2,1)S(1)} %get-tuple-element.12), channel_id=1, source_target_pairs={{0,1},{1,0},{2,3},{3,2},{4,5},{5,4},{6,7},{7,6},{8,9},{9,8},{10,11... | collective-permute-start | bytes 6193160 | tf_op jit(solution)/shard_map/ppermute | solution.py:388
  177.5 1.9 copy-start
  228.2 20.7 %all-to-all-start.3 = ((bf16[8,72,896]{2,1,0:T(8,128)(2,1)}), bf16[8,72,896]{2,1,0:T(8,128)(2,1)S(1)}, u32[]{:S(2)}, u32[]{:S(2)}) async-start(bf16[8,72,896]{2,1,0:T(8,128)(2,1)} %bitcast.7), calls=%async_computation.4 | async-start | bytes 2064384 | tf_op jit(solution)/shard_map/all_to_all | solution.py:478
  248.9 1.7 copy-start.1
  250.7 6.5 %collective-permute-start.2 = (bf16[72,896]{1,0:T(8,128)(2,1)S(1)}, bf16[72,896]{1,0:T(8,128)(2,1)S(1)}, u32[]{:S(2)}, u32[]{:S(2)}) collective-permute-start(bf16[72,896]{1,0:T(8,128)(2,1)S(1)} %shard_map.86), channel_id=1, source_target_pairs={{0,16},{16,0},{1,17},{17,1},{2,18},{18,2},{3,19},{19,3},{4,20},{20... | collective-permute-start | bytes 387080 | tf_op jit(solution)/shard_map/ppermute | solution.py:388
  257.3 6.2 %collective-permute-start.5 = (bf16[72,896]{1,0:T(8,128)(2,1)S(1)}, bf16[72,896]{1,0:T(8,128)(2,1)S(1)}, u32[]{:S(2)}, u32[]{:S(2)}) collective-permute-start(bf16[72,896]{1,0:T(8,128)(2,1)S(1)} %add_convert_fusion.refs_0_), channel_id=1, source_target_pairs={{0,96},{32,64},{64,32},{96,0},{1,97},{33,65},{65,33},{97,1},{2,98}... | collective-permute-start | bytes 387080 | tf_op jit(solution)/shard_map/ppermute | solution.py:481
  259.5 6.5 %collective-permute-start.4 = (bf16[72,896]{1,0:T(8,128)(2,1)S(1)}, bf16[72,896]{1,0:T(8,128)(2,1)S(1)}, u32[]{:S(2)}, u32[]{:S(2)}) collective-permute-start(bf16[72,896]{1,0:T(8,128)(2,1)S(1)} %add_convert_fusion.refs_0_), channel_id=1, source_target_pairs={{0,64},{32,96},{64,0},{96,32},{1,65},{33,97},{65,1},{97,33},{2,66}... | collective-permute-start | bytes 387080 | tf_op jit(solution)/shard_map/ppermute | solution.py:481
  259.6 6.3 %collective-permute-start.3 = (bf16[72,896]{1,0:T(8,128)(2,1)S(1)}, bf16[72,896]{1,0:T(8,128)(2,1)S(1)}, u32[]{:S(2)}, u32[]{:S(2)}) collective-permute-start(bf16[72,896]{1,0:T(8,128)(2,1)S(1)} %add_convert_fusion.refs_0_), channel_id=1, source_target_pairs={{0,32},{32,0},{64,96},{96,64},{1,33},{33,1},{65,97},{97,65},{2,34}... | collective-permute-start | bytes 387080 | tf_op jit(solution)/shard_map/ppermute | solution.py:481
Sparse Core Ops, SparseCore 0:
  179.6 48.5 reduce-scatter.1
where the time goes:
time: 274 us
  waiting for transfers between devices  125 us (46%)
  Pallas kernels  70.7 us (26%)
  blocking collectives  36.1 us (13%)
  starting transfers between devices  22.1 us (8%)
  between operations  14.1 us (5%)
  local copies, waits for them, and re-layouts  5.64 us (2%)
    all_to_all x1, waiting for transfers between devices, per_device(): received = lax.all_to_all(sent, SEQ, 0, 0, tiled=True)  103 us
    all_to_all x1, blocking collectives, per_device(): d_input = unpack(lax.all_to_all(d_local, SEQ, 0, 0, tiled=True))  36.1 us
    pallas_call x1, Pallas kernels, attend(): pl.pallas_call(functools.partial(attend_kernel, cells), in_specs=[vmem, p...  30.4 us
    pallas_call x1, Pallas kernels, input_grad(): pl.pallas_call(input_grad_kernel, grid=(rows // step - 1,), in_specs=[pl....  12.5 us
    all_to_all x1, waiting for transfers between devices, per_device(): share = fold(lax.all_to_all(over_z, ('y', 'xl'), 0, 0, tiled=True), d_input)  11.7 us
    pallas_call x2, Pallas kernels, pack(): pl.pallas_call(functools.partial(pack_kernel, cells, group), grid=(device...  11.4 us
    pallas_call x2, Pallas kernels, product(): pl.pallas_call(product_kernel, in_specs=[vmem] * (1 + len(ranges)), out_s...  6.73 us
    ppermute x3, waiting for transfers between devices, swap(): return lax.ppermute(value, axis, [(0, 1), (1, 0)])  5.86 us
  transfers between devices with their start and end apart: 10, of which 8 were waited for; matrix products, arithmetic and copies ran while one was open for 0% of the time, Pallas kernels for 20%

commit v1 on v0

--- a/solution.py
+++ b/solution.py
@@ -32,7 +32,7 @@
 
 def pack(arrays, devices):
     frames, cells = arrays[0].shape[1], arrays[0].shape[2] // devices
-    group = 4
+    group = 8
     block = pl.BlockSpec((1, frames, group * cells, WIDTH), lambda j: (0, 0, j, 0))
     count = len(arrays)
     return pl.pallas_call(

time: 274 us -> 273 us (level)
  no operation moved by 1% of the time
where the time goes in v1:
time: 273 us
  waiting for transfers between devices  126 us (46%)
  Pallas kernels  68.5 us (25%)
  blocking collectives  36.1 us (13%)
  starting transfers between devices  22.1 us (8%)
  between operations  14.1 us (5%)
  local copies, waits for them, and re-layouts  5.64 us (2%)
    all_to_all x1, waiting for transfers between devices, per_device(): received = lax.all_to_all(sent, SEQ, 0, 0, tiled=True)  104 us
    all_to_all x1, blocking collectives, per_device(): d_input = unpack(lax.all_to_all(d_local, SEQ, 0, 0, tiled=True))  36.1 us
    pallas_call x1, Pallas kernels, attend(): pl.pallas_call(functools.partial(attend_kernel, cells), in_specs=[vmem, p...  30.4 us
    pallas_call x1, Pallas kernels, input_grad(): pl.pallas_call(input_grad_kernel, grid=(rows // step - 1,), in_specs=[pl....  12.5 us
    all_to_all x1, waiting for transfers between devices, per_device(): share = fold(lax.all_to_all(over_z, ('y', 'xl'), 0, 0, tiled=True), d_input)  11.7 us
    pallas_call x2, Pallas kernels, pack(): pl.pallas_call(functools.partial(pack_kernel, cells, group), grid=(device...  9.19 us
    pallas_call x2, Pallas kernels, product(): pl.pallas_call(product_kernel, in_specs=[vmem] * (1 + len(ranges)), out_s...  6.73 us
    ppermute x3, waiting for transfers between devices, swap(): return lax.ppermute(value, axis, [(0, 1), (1, 0)])  5.88 us
  transfers between devices with their start and end apart: 10, of which 8 were waited for; matrix products, arithmetic and copies ran while one was open for 0% of the time, Pallas kernels for 20%

profile of v1, /device:TPU:0, one launch (start us, length us, event | category | flops | bytes accessed | tf_op | source)
XLA Modules:
  0.0 272.7 jit_solution(14986324508317215096)
XLA Ops:
  7.2 6.4 %shard_map.77 = bf16[16,4,4,16,1152]{4,3,2,1,0:T(8,128)(2,1)} custom-call(bf16[1,4,256,1152]{3,2,1,0:T(8,128)(2,1)} %refs_0_.2, bf16[1,4,256,1152]{3,2,1,0:T(8,128)(2,1)} %refs_1_.1, bf16[1,4,256,1152]{3,2,1,0:T(8,128)(2,1)} %refs_2_.1, bf16[1,4,256,1152]{3,2,1,0:T(8,128)(2,1)} %refs_3_.1), custom_call_target="tpu_custom_call" | custom-call | bytes 18874368 | tf_op jit(solution)/shard_map/pallas_call | solution.py:38
  13.6 5.6 %all-to-all-start = ((bf16[16,4,4,16,1152]{4,3,2,1,0:T(8,128)(2,1)}), bf16[16,4,4,16,1152]{4,3,2,1,0:T(8,128)(2,1)}, u32[]{:S(2)}, u32[]{:S(2)}) async-start(bf16[16,4,4,16,1152]{4,3,2,1,0:T(8,128)(2,1)} %shard_map.77), calls=%async_computation | async-start | bytes 18874368 | tf_op jit(solution)/shard_map/all_to_all | solution.py:459
  19.2 2.8 %shard_map.79 = bf16[16,1,4,16,1152]{4,3,2,1,0:T(8,128)(2,1)} custom-call(bf16[1,4,256,1152]{3,2,1,0:T(8,128)(2,1)} %refs_0_.3), custom_call_target="tpu_custom_call" | custom-call | bytes 4718592 | tf_op jit(solution)/shard_map/pallas_call | solution.py:38
  22.0 103.8 %all-to-all-done.r_ref = bf16[16,4,4,16,1152]{4,3,2,1,0:T(8,128)(2,1)} async-done(((bf16[16,4,4,16,1152]{4,3,2,1,0:T(8,128)(2,1)}), bf16[16,4,4,16,1152]{4,3,2,1,0:T(8,128)(2,1)}, u32[]{:S(2)}, u32[]{:S(2)}) %all-to-all-start) | async-done | bytes 9437216 | tf_op jit(solution)/shard_map/all_to_all | solution.py:459
  125.8 3.7 %all-to-all-start.1 = ((bf16[16,1,4,16,1152]{4,3,2,1,0:T(8,128)(2,1)}), bf16[16,1,4,16,1152]{4,3,2,1,0:T(8,128)(2,1)S(1)}, u32[]{:S(2)}, u32[]{:S(2)}) async-start(bf16[16,1,4,16,1152]{4,3,2,1,0:T(8,128)(2,1)} %shard_map.79), calls=%async_computation.1 | async-start | bytes 4718592 | tf_op jit(solution)/shard_map/all_to_all | solution.py:461
  129.5 0.0 reduce-scatter.2.cloned.1.call-start
  129.6 30.4 %shard_map.78 = (bf16[1024,1792]{1,0:T(8,128)(2,1)}, bf16[1024,1664]{1,0:T(8,128)(2,1)}, bf16[1024,1152]{1,0:T(8,128)(2,1)}) custom-call(bf16[16,4,4,16,1152]{4,3,2,1,0:T(8,128)(2,1)} %all-to-all-done.r_ref, bf16[1152,3456]{1,0:T(8,128)(2,1)} %w_ref.1), custom_call_target="tpu_custom_call" | custom-call | flops 24000000000 | bytes 16515072 | tf_op jit(solution)/shard_map/pallas_call | solution.py:209
  160.0 0.2 all-to-all-done.1
  160.2 0.0 copy-start.3
  160.2 2.0 copy-done.3
  162.2 0.0 copy-start.2
  162.2 3.6 %shard_map.80 = (bf16[2,8,72,896]{3,2,1,0:T(8,128)(2,1)S(1)}, bf16[576,1024]{1,0:T(8,128)(2,1)S(1)}, bf16[576,1024]{1,0:T(8,128)(2,1)S(1)}) custom-call(s32[1]{0:T(128)} %bitcast.core_ref, bf16[1024,1152]{1,0:T(8,128)(2,1)S(1)} %bitcast.5, bf16[1024,1792]{1,0:T(8,128)(2,1)S(1)} %copy-done.3), custom_call_target="tpu_custom_call" | custom-call | flops 2113929216 | bytes 8093696 | tf_op jit(solution)/shard_map/pallas_call | solution.py:313
  165.9 0.0 copy-done.2
  165.9 0.0 copy-start.4
  165.9 2.3 shard_map.82
  168.2 0.2 collective-permute-start.1
  168.4 0.4 collective-permute-start
  168.8 0.0 copy-done.4
  168.8 4.4 %shard_map.81.own_ref = bf16[4,8,72,896]{3,2,1,0:T(8,128)(2,1)S(1)} custom-call(bf16[576,1024]{1,0:T(8,128)(2,1)S(1)} %get-tuple-element.11.turned_ref, bf16[1024,1792]{1,0:T(8,128)(2,1)S(1)} %copy-done.4, bf16[1024,1664]{1,0:T(8,128)(2,1)S(1)} %copy-done.2), custom_call_target="tpu_custom_call" | custom-call | flops 4227858432 | bytes 12648448 | tf_op jit(solution)/shard_map/pallas_call | solution.py:339
  173.2 0.0 collective-permute-done.1.late_ref
  173.2 2.1 collective-permute-done.early_ref
  175.3 1.0 shard_map.83.after_ref
  176.4 0.0 copy-start
  176.4 1.9 copy-done
  178.3 0.0 reduce-scatter.2.cloned.1.call-update
  178.3 12.5 %shard_map.84 = bf16[1024,1152]{1,0:T(8,128)(2,1)} custom-call(bf16[1024,1792]{1,0:T(8,128)(2,1)} %get-tuple-element.8.g_ref.refs_0_.g0_ref, bf16[1024,1664]{1,0:T(8,128)(2,1)} %get-tuple-element.9.refs_1_.refs_0_.g1_ref, bf16[1152,3456]{1,0:T(8,128)(2,1)} %w_ref.1, bf16[1024,1152]{1,0:T(8,128)(2,1)} %get-tuple-element.10.early_ref, ...), custom_call_target="tpu_custom_call", output_to_operand_aliasing={{}: (3, {})} | custom-call | flops 8153726976 | bytes 15040512 | tf_op jit(solution)/shard_map/pallas_call | solution.py:241
  190.8 36.1 %all_to_all.20.in_ref = bf16[16,4,16,1152]{3,2,1,0:T(8,128)(2,1)} all-to-all(bf16[16,4,16,1152]{3,2,1,0:T(8,128)(2,1)} %bitcast.6), channel_id=1, replica_groups=mesh['z'=4,'xh'=2,'y'=4,'xl'=2,'core'=2] {'y','xl','core'}, dimensions={0} | all-to-all | bytes 4718592 | tf_op jit(solution)/shard_map/all_to_all | solution.py:476
  226.8 0.2 reduce-scatter.2.cloned.1.call-done
  227.1 5.2 %all-to-all-start.3 = ((bf16[8,72,896]{2,1,0:T(8,128)(2,1)}), bf16[8,72,896]{2,1,0:T(8,128)(2,1)S(1)}, u32[]{:S(2)}, u32[]{:S(2)}) async-start(bf16[8,72,896]{2,1,0:T(8,128)(2,1)} %bitcast.7), calls=%async_computation.4 | async-start | bytes 2064384 | tf_op jit(solution)/shard_map/all_to_all | solution.py:478
  232.2 3.9 %shard_map.85.after_ref = bf16[1,4,256,1152]{3,2,1,0:T(8,128)(2,1)} custom-call(bf16[16,4,16,1152]{3,2,1,0:T(8,128)(2,1)} %all_to_all.20.in_ref), custom_call_target="tpu_custom_call" | custom-call | bytes 4718592 | tf_op jit(solution)/shard_map/pallas_call | solution.py:59
  236.1 11.7 %all-to-all-done.3.blocks_ref = bf16[8,72,896]{2,1,0:T(8,128)(2,1)S(1)} async-done(((bf16[8,72,896]{2,1,0:T(8,128)(2,1)}), bf16[8,72,896]{2,1,0:T(8,128)(2,1)S(1)}, u32[]{:S(2)}, u32[]{:S(2)}) %all-to-all-start.3) | async-done | bytes 1032224 | tf_op jit(solution)/shard_map/all_to_all | solution.py:478
  247.8 0.0 copy-start.1
  247.8 1.7 copy-done.1
  249.5 0.1 shard_map.86
  249.6 2.8 %collective-permute-start.2 = (bf16[72,896]{1,0:T(8,128)(2,1)S(1)}, bf16[72,896]{1,0:T(8,128)(2,1)S(1)}, u32[]{:S(2)}, u32[]{:S(2)}) collective-permute-start(bf16[72,896]{1,0:T(8,128)(2,1)S(1)} %shard_map.86), channel_id=1, source_target_pairs={{0,16},{16,0},{1,17},{17,1},{2,18},{18,2},{3,19},{19,3},{4,20},{20... | collective-permute-start | bytes 387080 | tf_op jit(solution)/shard_map/ppermute | solution.py:388
  252.4 3.8 %collective-permute-done.2 = bf16[72,896]{1,0:T(8,128)(2,1)S(1)} collective-permute-done((bf16[72,896]{1,0:T(8,128)(2,1)S(1)}, bf16[72,896]{1,0:T(8,128)(2,1)S(1)}, u32[]{:S(2)}, u32[]{:S(2)}) %collective-permute-start.2) | collective-permute-done | bytes 129056 | tf_op jit(solution)/shard_map/ppermute | solution.py:388
  256.2 2.1 collective-permute-start.5
  258.3 0.2 collective-permute-start.4
  258.5 1.9 collective-permute-start.3
  260.4 2.1 collective-permute-done.5.refs_3_
  262.4 2.3 collective-permute-done.4.refs_2_
  264.8 0.0 collective-permute-done.3.refs_1_
  264.8 1.0 shard_map.87
  (1 shorter events, 0.0 us)
Async XLA Ops:
  13.6 112.2 %all-to-all-start = ((bf16[16,4,4,16,1152]{4,3,2,1,0:T(8,128)(2,1)}), bf16[16,4,4,16,1152]{4,3,2,1,0:T(8,128)(2,1)}, u32[]{:S(2)}, u32[]{:S(2)}) async-start(bf16[16,4,4,16,1152]{4,3,2,1,0:T(8,128)(2,1)} %shard_map.77), calls=%async_computation | async-start | bytes 18874368 | tf_op jit(solution)/shard_map/all_to_all | solution.py:459
  125.8 34.4 %all-to-all-start.1 = ((bf16[16,1,4,16,1152]{4,3,2,1,0:T(8,128)(2,1)}), bf16[16,1,4,16,1152]{4,3,2,1,0:T(8,128)(2,1)S(1)}, u32[]{:S(2)}, u32[]{:S(2)}) async-start(bf16[16,1,4,16,1152]{4,3,2,1,0:T(8,128)(2,1)} %shard_map.79), calls=%async_computation.1 | async-start | bytes 4718592 | tf_op jit(solution)/shard_map/all_to_all | solution.py:461
  129.5 97.5 %reduce-scatter.2.cloned.1.call-start = ((), (), s32[]{:S(2)}) async-start(), calls=%async_computation.5 | async-start | bytes 5160960 | tf_op jit(solution)/shard_map/reduce_scatter | solution.py:473
  160.2 2.0 copy-start.3
  162.2 3.6 %copy-start.2 = (bf16[1024,1664]{1,0:T(8,128)(2,1)S(1)}, bf16[1024,1664]{1,0:T(8,128)(2,1)}, u32[]{:S(2)}) copy-start(bf16[1024,1664]{1,0:T(8,128)(2,1)} %get-tuple-element.9.refs_1_.refs_0_.g1_ref) | copy-start | bytes 10223620
  165.9 2.9 %copy-start.4 = (bf16[1024,1792]{1,0:T(8,128)(2,1)S(1)}, bf16[1024,1792]{1,0:T(8,128)(2,1)}, u32[]{:S(2)}) copy-start(bf16[1024,1792]{1,0:T(8,128)(2,1)} %get-tuple-element.8.g_ref.refs_0_.g0_ref) | copy-start | bytes 11010052
  168.2 5.0 %collective-permute-start.1 = (bf16[2,8,72,896]{3,2,1,0:T(8,128)(2,1)S(1)}, bf16[2,8,72,896]{3,2,1,0:T(8,128)(2,1)S(1)}, u32[]{:S(2)}, u32[]{:S(2)}) collective-permute-start(bf16[2,8,72,896]{3,2,1,0:T(8,128)(2,1)S(1)} %shard_map.82), channel_id=1, source_target_pairs={{0,1},{1,0},{2,3},{3,2},{4,5},{5,4},{6,7},{7,6},{8,9},{9,8},{10,11... | collective-permute-start | bytes 6193160 | tf_op jit(solution)/shard_map/ppermute | solution.py:388
  168.4 7.0 %collective-permute-start = (bf16[2,8,72,896]{3,2,1,0:T(8,128)(2,1)S(1)}, bf16[2,8,72,896]{3,2,1,0:T(8,128)(2,1)S(1)}, u32[]{:S(2)}, u32[]{:S(2)}) collective-permute-start(bf16[2,8,72,896]{3,2,1,0:T(8,128)(2,1)S(1)} %get-tuple-element.12), channel_id=1, source_target_pairs={{0,1},{1,0},{2,3},{3,2},{4,5},{5,4},{6,7},{7,6},{8,9},{9,8},{10,11... | collective-permute-start | bytes 6193160 | tf_op jit(solution)/shard_map/ppermute | solution.py:388
  176.4 1.9 copy-start
  227.1 20.8 %all-to-all-start.3 = ((bf16[8,72,896]{2,1,0:T(8,128)(2,1)}), bf16[8,72,896]{2,1,0:T(8,128)(2,1)S(1)}, u32[]{:S(2)}, u32[]{:S(2)}) async-start(bf16[8,72,896]{2,1,0:T(8,128)(2,1)} %bitcast.7), calls=%async_computation.4 | async-start | bytes 2064384 | tf_op jit(solution)/shard_map/all_to_all | solution.py:478
  247.8 1.7 copy-start.1
  249.6 6.5 %collective-permute-start.2 = (bf16[72,896]{1,0:T(8,128)(2,1)S(1)}, bf16[72,896]{1,0:T(8,128)(2,1)S(1)}, u32[]{:S(2)}, u32[]{:S(2)}) collective-permute-start(bf16[72,896]{1,0:T(8,128)(2,1)S(1)} %shard_map.86), channel_id=1, source_target_pairs={{0,16},{16,0},{1,17},{17,1},{2,18},{18,2},{3,19},{19,3},{4,20},{20... | collective-permute-start | bytes 387080 | tf_op jit(solution)/shard_map/ppermute | solution.py:388
  256.2 6.2 %collective-permute-start.5 = (bf16[72,896]{1,0:T(8,128)(2,1)S(1)}, bf16[72,896]{1,0:T(8,128)(2,1)S(1)}, u32[]{:S(2)}, u32[]{:S(2)}) collective-permute-start(bf16[72,896]{1,0:T(8,128)(2,1)S(1)} %add_convert_fusion.refs_0_), channel_id=1, source_target_pairs={{0,96},{32,64},{64,32},{96,0},{1,97},{33,65},{65,33},{97,1},{2,98}... | collective-permute-start | bytes 387080 | tf_op jit(solution)/shard_map/ppermute | solution.py:481
  258.3 6.5 %collective-permute-start.4 = (bf16[72,896]{1,0:T(8,128)(2,1)S(1)}, bf16[72,896]{1,0:T(8,128)(2,1)S(1)}, u32[]{:S(2)}, u32[]{:S(2)}) collective-permute-start(bf16[72,896]{1,0:T(8,128)(2,1)S(1)} %add_convert_fusion.refs_0_), channel_id=1, source_target_pairs={{0,64},{32,96},{64,0},{96,32},{1,65},{33,97},{65,1},{97,33},{2,66}... | collective-permute-start | bytes 387080 | tf_op jit(solution)/shard_map/ppermute | solution.py:481
  258.5 6.3 %collective-permute-start.3 = (bf16[72,896]{1,0:T(8,128)(2,1)S(1)}, bf16[72,896]{1,0:T(8,128)(2,1)S(1)}, u32[]{:S(2)}, u32[]{:S(2)}) collective-permute-start(bf16[72,896]{1,0:T(8,128)(2,1)S(1)} %add_convert_fusion.refs_0_), channel_id=1, source_target_pairs={{0,32},{32,0},{64,96},{96,64},{1,33},{33,1},{65,97},{97,65},{2,34}... | collective-permute-start | bytes 387080 | tf_op jit(solution)/shard_map/ppermute | solution.py:481
Sparse Core Ops, SparseCore 0:
  178.5 48.5 reduce-scatter.1

commit v2 on v1

--- a/solution.py
+++ b/solution.py
@@ -62,7 +62,7 @@
         in_specs=[pl.BlockSpec((group, frames, cells, width), lambda j: (j, 0, 0, 0))],
         out_specs=pl.BlockSpec((1, frames, group * cells, width), lambda j: (0, 0, j, 0)),
         out_shape=jax.ShapeDtypeStruct((1, frames, cells * devices, width), jnp.bfloat16),
-        compiler_params=pltpu.CompilerParams(vmem_limit_bytes=60 * MIB),
+        compiler_params=pltpu.CompilerParams(vmem_limit_bytes=20 * MIB),
         cost_estimate=pl.CostEstimate(flops=0, bytes_accessed=4 * blocks.size, transcendentals=0),
     )(blocks)
 
@@ -324,7 +324,7 @@
             pltpu.VMEM((2, half, rows // chunks), jnp.float32),
             pltpu.SemaphoreType.DMA((chunks,)),
         ],
-        compiler_params=pltpu.CompilerParams(vmem_limit_bytes=36 * MIB),
+        compiler_params=pltpu.CompilerParams(vmem_limit_bytes=24 * MIB),
         cost_estimate=pl.CostEstimate(
             flops=rows * WIDTH * step * parts,
             bytes_accessed=rows * (2 * WIDTH + 2 * step * parts) + WIDTH * step * parts,
@@ -341,7 +341,7 @@
         in_specs=[vmem] * (1 + len(ranges)),
         out_specs=vmem,
         out_shape=jax.ShapeDtypeStruct((parts, owners, half // owners, step), jnp.bfloat16),
-        compiler_params=pltpu.CompilerParams(vmem_limit_bytes=36 * MIB),
+        compiler_params=pltpu.CompilerParams(vmem_limit_bytes=24 * MIB),
         cost_estimate=pl.CostEstimate(
             flops=rows * WIDTH * step * parts,
             bytes_accessed=rows * (WIDTH + 2 * step * parts) + WIDTH * step * parts,
@@ -377,7 +377,7 @@
         ],
         out_specs=pl.BlockSpec(block, lambda j: (j, 0, 0, 0)),
         out_shape=jax.ShapeDtypeStruct(own.shape, own.dtype),
-        compiler_params=pltpu.CompilerParams(vmem_limit_bytes=36 * MIB),
+        compiler_params=pltpu.CompilerParams(vmem_limit_bytes=24 * MIB),
         cost_estimate=pl.CostEstimate(
             flops=own.size, bytes_accessed=6 * own.size, transcendentals=0
         ),

time: 273 us -> 273 us (level)
  transfers between devices with their start and end apart: 10 -> 10, of which waited for: 8 -> 8; matrix products, arithmetic and copies ran while one was open for 0% -> 0% of each run, Pallas kernels for 20% -> 19%
where the time goes in v2:
time: 273 us
  waiting for transfers between devices  128 us (47%)
  Pallas kernels  66.5 us (24%)
  blocking collectives  36 us (13%)
  starting transfers between devices  22.1 us (8%)
  between operations  14.1 us (5%)
  local copies, waits for them, and re-layouts  5.64 us (2%)
    all_to_all x1, waiting for transfers between devices, per_device(): received = lax.all_to_all(sent, SEQ, 0, 0, tiled=True)  104 us
    all_to_all x1, blocking collectives, per_device(): d_input = unpack(lax.all_to_all(d_local, SEQ, 0, 0, tiled=True))  36 us
    pallas_call x1, Pallas kernels, attend(): pl.pallas_call(functools.partial(attend_kernel, cells), in_specs=[vmem, p...  30.4 us
    all_to_all x1, waiting for transfers between devices, per_device(): share = fold(lax.all_to_all(over_z, ('y', 'xl'), 0, 0, tiled=True), d_input)  13.7 us
    pallas_call x1, Pallas kernels, input_grad(): pl.pallas_call(input_grad_kernel, grid=(rows // step - 1,), in_specs=[pl....  12.5 us
    pallas_call x2, Pallas kernels, pack(): pl.pallas_call(functools.partial(pack_kernel, cells, group), grid=(device...  9.19 us
    pallas_call x2, Pallas kernels, product(): pl.pallas_call(product_kernel, in_specs=[vmem] * (1 + len(ranges)), out_s...  6.73 us
    ppermute x3, waiting for transfers between devices, swap(): return lax.ppermute(value, axis, [(0, 1), (1, 0)])  5.88 us
  transfers between devices with their start and end apart: 10, of which 8 were waited for; matrix products, arithmetic and copies ran while one was open for 0% of the time, Pallas kernels for 19%

profile of v2, /device:TPU:0, one launch (start us, length us, event | category | flops | bytes accessed | tf_op | source)
XLA Modules:
  0.0 272.6 jit_solution(14408815218772598383)
XLA Ops:
  7.2 6.4 %shard_map.77 = bf16[16,4,4,16,1152]{4,3,2,1,0:T(8,128)(2,1)} custom-call(bf16[1,4,256,1152]{3,2,1,0:T(8,128)(2,1)} %refs_0_.2, bf16[1,4,256,1152]{3,2,1,0:T(8,128)(2,1)} %refs_1_.1, bf16[1,4,256,1152]{3,2,1,0:T(8,128)(2,1)} %refs_2_.1, bf16[1,4,256,1152]{3,2,1,0:T(8,128)(2,1)} %refs_3_.1), custom_call_target="tpu_custom_call" | custom-call | bytes 18874368 | tf_op jit(solution)/shard_map/pallas_call | solution.py:38
  13.6 5.6 %all-to-all-start = ((bf16[16,4,4,16,1152]{4,3,2,1,0:T(8,128)(2,1)}), bf16[16,4,4,16,1152]{4,3,2,1,0:T(8,128)(2,1)}, u32[]{:S(2)}, u32[]{:S(2)}) async-start(bf16[16,4,4,16,1152]{4,3,2,1,0:T(8,128)(2,1)} %shard_map.77), calls=%async_computation | async-start | bytes 18874368 | tf_op jit(solution)/shard_map/all_to_all | solution.py:459
  19.2 2.8 %shard_map.79 = bf16[16,1,4,16,1152]{4,3,2,1,0:T(8,128)(2,1)} custom-call(bf16[1,4,256,1152]{3,2,1,0:T(8,128)(2,1)} %refs_0_.3), custom_call_target="tpu_custom_call" | custom-call | bytes 4718592 | tf_op jit(solution)/shard_map/pallas_call | solution.py:38
  22.0 103.8 %all-to-all-done.r_ref = bf16[16,4,4,16,1152]{4,3,2,1,0:T(8,128)(2,1)} async-done(((bf16[16,4,4,16,1152]{4,3,2,1,0:T(8,128)(2,1)}), bf16[16,4,4,16,1152]{4,3,2,1,0:T(8,128)(2,1)}, u32[]{:S(2)}, u32[]{:S(2)}) %all-to-all-start) | async-done | bytes 9437216 | tf_op jit(solution)/shard_map/all_to_all | solution.py:459
  125.8 3.7 %all-to-all-start.1 = ((bf16[16,1,4,16,1152]{4,3,2,1,0:T(8,128)(2,1)}), bf16[16,1,4,16,1152]{4,3,2,1,0:T(8,128)(2,1)S(1)}, u32[]{:S(2)}, u32[]{:S(2)}) async-start(bf16[16,1,4,16,1152]{4,3,2,1,0:T(8,128)(2,1)} %shard_map.79), calls=%async_computation.1 | async-start | bytes 4718592 | tf_op jit(solution)/shard_map/all_to_all | solution.py:461
  129.5 0.0 reduce-scatter.2.cloned.1.call-start
  129.6 30.4 %shard_map.78 = (bf16[1024,1792]{1,0:T(8,128)(2,1)}, bf16[1024,1664]{1,0:T(8,128)(2,1)}, bf16[1024,1152]{1,0:T(8,128)(2,1)}) custom-call(bf16[16,4,4,16,1152]{4,3,2,1,0:T(8,128)(2,1)} %all-to-all-done.r_ref, bf16[1152,3456]{1,0:T(8,128)(2,1)} %w_ref.1), custom_call_target="tpu_custom_call" | custom-call | flops 24000000000 | bytes 16515072 | tf_op jit(solution)/shard_map/pallas_call | solution.py:209
  160.0 0.2 all-to-all-done.1
  160.2 0.0 copy-start.3
  160.2 2.0 copy-done.3
  162.2 0.0 copy-start.2
  162.2 3.6 %shard_map.80 = (bf16[2,8,72,896]{3,2,1,0:T(8,128)(2,1)S(1)}, bf16[576,1024]{1,0:T(8,128)(2,1)S(1)}, bf16[576,1024]{1,0:T(8,128)(2,1)S(1)}) custom-call(s32[1]{0:T(128)} %bitcast.core_ref, bf16[1024,1152]{1,0:T(8,128)(2,1)S(1)} %bitcast.5, bf16[1024,1792]{1,0:T(8,128)(2,1)S(1)} %copy-done.3), custom_call_target="tpu_custom_call" | custom-call | flops 2113929216 | bytes 8093696 | tf_op jit(solution)/shard_map/pallas_call | solution.py:313
  165.9 0.0 copy-done.2
  165.9 0.0 copy-start.4
  165.9 2.3 shard_map.82
  168.2 0.2 collective-permute-start.1
  168.4 0.4 collective-permute-start
  168.8 0.0 copy-done.4
  168.8 4.4 %shard_map.81.own_ref = bf16[4,8,72,896]{3,2,1,0:T(8,128)(2,1)S(1)} custom-call(bf16[576,1024]{1,0:T(8,128)(2,1)S(1)} %get-tuple-element.11.turned_ref, bf16[1024,1792]{1,0:T(8,128)(2,1)S(1)} %copy-done.4, bf16[1024,1664]{1,0:T(8,128)(2,1)S(1)} %copy-done.2), custom_call_target="tpu_custom_call" | custom-call | flops 4227858432 | bytes 12648448 | tf_op jit(solution)/shard_map/pallas_call | solution.py:339
  173.2 0.0 collective-permute-done.1.late_ref
  173.2 2.1 collective-permute-done.early_ref
  175.3 1.0 shard_map.83.after_ref
  176.4 0.0 copy-start
  176.4 1.9 copy-done
  178.3 0.0 reduce-scatter.2.cloned.1.call-update
  178.3 12.5 %shard_map.84 = bf16[1024,1152]{1,0:T(8,128)(2,1)} custom-call(bf16[1024,1792]{1,0:T(8,128)(2,1)} %get-tuple-element.8.g_ref.refs_0_.g0_ref, bf16[1024,1664]{1,0:T(8,128)(2,1)} %get-tuple-element.9.refs_1_.refs_0_.g1_ref, bf16[1152,3456]{1,0:T(8,128)(2,1)} %w_ref.1, bf16[1024,1152]{1,0:T(8,128)(2,1)} %get-tuple-element.10.early_ref, ...), custom_call_target="tpu_custom_call", output_to_operand_aliasing={{}: (3, {})} | custom-call | flops 8153726976 | bytes 15040512 | tf_op jit(solution)/shard_map/pallas_call | solution.py:241
  190.8 36.0 %all_to_all.20.in_ref = bf16[16,4,16,1152]{3,2,1,0:T(8,128)(2,1)S(1)} all-to-all(bf16[16,4,16,1152]{3,2,1,0:T(8,128)(2,1)} %bitcast.6), channel_id=1, replica_groups=mesh['z'=4,'xh'=2,'y'=4,'xl'=2,'core'=2] {'y','xl','core'}, dimensions={0} | all-to-all | bytes 4718592 | tf_op jit(solution)/shard_map/all_to_all | solution.py:476
  226.7 0.3 reduce-scatter.2.cloned.1.call-done
  227.1 5.2 %all-to-all-start.3 = ((bf16[8,72,896]{2,1,0:T(8,128)(2,1)}), bf16[8,72,896]{2,1,0:T(8,128)(2,1)S(1)}, u32[]{:S(2)}, u32[]{:S(2)}) async-start(bf16[8,72,896]{2,1,0:T(8,128)(2,1)} %bitcast.7), calls=%async_computation.4 | async-start | bytes 2064384 | tf_op jit(solution)/shard_map/all_to_all | solution.py:478
  232.2 1.9 shard_map.85.after_ref
  234.2 13.7 %all-to-all-done.3.blocks_ref = bf16[8,72,896]{2,1,0:T(8,128)(2,1)S(1)} async-done(((bf16[8,72,896]{2,1,0:T(8,128)(2,1)}), bf16[8,72,896]{2,1,0:T(8,128)(2,1)S(1)}, u32[]{:S(2)}, u32[]{:S(2)}) %all-to-all-start.3) | async-done | bytes 1032224 | tf_op jit(solution)/shard_map/all_to_all | solution.py:478
  247.8 0.0 copy-start.1
  247.8 1.7 copy-done.1
  249.5 0.1 shard_map.86
  249.6 2.8 %collective-permute-start.2 = (bf16[72,896]{1,0:T(8,128)(2,1)S(1)}, bf16[72,896]{1,0:T(8,128)(2,1)S(1)}, u32[]{:S(2)}, u32[]{:S(2)}) collective-permute-start(bf16[72,896]{1,0:T(8,128)(2,1)S(1)} %shard_map.86), channel_id=1, source_target_pairs={{0,16},{16,0},{1,17},{17,1},{2,18},{18,2},{3,19},{19,3},{4,20},{20... | collective-permute-start | bytes 387080 | tf_op jit(solution)/shard_map/ppermute | solution.py:388
  252.4 3.8 %collective-permute-done.2 = bf16[72,896]{1,0:T(8,128)(2,1)S(1)} collective-permute-done((bf16[72,896]{1,0:T(8,128)(2,1)S(1)}, bf16[72,896]{1,0:T(8,128)(2,1)S(1)}, u32[]{:S(2)}, u32[]{:S(2)}) %collective-permute-start.2) | collective-permute-done | bytes 129056 | tf_op jit(solution)/shard_map/ppermute | solution.py:388
  256.2 2.0 collective-permute-start.5
  258.2 0.3 collective-permute-start.4
  258.5 1.9 collective-permute-start.3
  260.4 2.1 collective-permute-done.5.refs_3_
  262.4 2.2 collective-permute-done.4.refs_2_
  264.7 0.0 collective-permute-done.3.refs_1_
  264.7 1.0 shard_map.87
  (1 shorter events, 0.0 us)
Async XLA Ops:
  13.6 112.2 %all-to-all-start = ((bf16[16,4,4,16,1152]{4,3,2,1,0:T(8,128)(2,1)}), bf16[16,4,4,16,1152]{4,3,2,1,0:T(8,128)(2,1)}, u32[]{:S(2)}, u32[]{:S(2)}) async-start(bf16[16,4,4,16,1152]{4,3,2,1,0:T(8,128)(2,1)} %shard_map.77), calls=%async_computation | async-start | bytes 18874368 | tf_op jit(solution)/shard_map/all_to_all | solution.py:459
  125.8 34.4 %all-to-all-start.1 = ((bf16[16,1,4,16,1152]{4,3,2,1,0:T(8,128)(2,1)}), bf16[16,1,4,16,1152]{4,3,2,1,0:T(8,128)(2,1)S(1)}, u32[]{:S(2)}, u32[]{:S(2)}) async-start(bf16[16,1,4,16,1152]{4,3,2,1,0:T(8,128)(2,1)} %shard_map.79), calls=%async_computation.1 | async-start | bytes 4718592 | tf_op jit(solution)/shard_map/all_to_all | solution.py:461
  129.5 97.5 %reduce-scatter.2.cloned.1.call-start = ((), (), s32[]{:S(2)}) async-start(), calls=%async_computation.5 | async-start | bytes 5160960 | tf_op jit(solution)/shard_map/reduce_scatter | solution.py:473
  160.2 2.0 copy-start.3
  162.2 3.6 %copy-start.2 = (bf16[1024,1664]{1,0:T(8,128)(2,1)S(1)}, bf16[1024,1664]{1,0:T(8,128)(2,1)}, u32[]{:S(2)}) copy-start(bf16[1024,1664]{1,0:T(8,128)(2,1)} %get-tuple-element.9.refs_1_.refs_0_.g1_ref) | copy-start | bytes 10223620
  165.9 2.9 %copy-start.4 = (bf16[1024,1792]{1,0:T(8,128)(2,1)S(1)}, bf16[1024,1792]{1,0:T(8,128)(2,1)}, u32[]{:S(2)}) copy-start(bf16[1024,1792]{1,0:T(8,128)(2,1)} %get-tuple-element.8.g_ref.refs_0_.g0_ref) | copy-start | bytes 11010052
  168.2 5.0 %collective-permute-start.1 = (bf16[2,8,72,896]{3,2,1,0:T(8,128)(2,1)S(1)}, bf16[2,8,72,896]{3,2,1,0:T(8,128)(2,1)S(1)}, u32[]{:S(2)}, u32[]{:S(2)}) collective-permute-start(bf16[2,8,72,896]{3,2,1,0:T(8,128)(2,1)S(1)} %shard_map.82), channel_id=1, source_target_pairs={{0,1},{1,0},{2,3},{3,2},{4,5},{5,4},{6,7},{7,6},{8,9},{9,8},{10,11... | collective-permute-start | bytes 6193160 | tf_op jit(solution)/shard_map/ppermute | solution.py:388
  168.4 7.0 %collective-permute-start = (bf16[2,8,72,896]{3,2,1,0:T(8,128)(2,1)S(1)}, bf16[2,8,72,896]{3,2,1,0:T(8,128)(2,1)S(1)}, u32[]{:S(2)}, u32[]{:S(2)}) collective-permute-start(bf16[2,8,72,896]{3,2,1,0:T(8,128)(2,1)S(1)} %get-tuple-element.12), channel_id=1, source_target_pairs={{0,1},{1,0},{2,3},{3,2},{4,5},{5,4},{6,7},{7,6},{8,9},{9,8},{10,11... | collective-permute-start | bytes 6193160 | tf_op jit(solution)/shard_map/ppermute | solution.py:388
  176.4 1.9 copy-start
  227.1 20.8 %all-to-all-start.3 = ((bf16[8,72,896]{2,1,0:T(8,128)(2,1)}), bf16[8,72,896]{2,1,0:T(8,128)(2,1)S(1)}, u32[]{:S(2)}, u32[]{:S(2)}) async-start(bf16[8,72,896]{2,1,0:T(8,128)(2,1)} %bitcast.7), calls=%async_computation.4 | async-start | bytes 2064384 | tf_op jit(solution)/shard_map/all_to_all | solution.py:478
  247.8 1.7 copy-start.1
  249.6 6.5 %collective-permute-start.2 = (bf16[72,896]{1,0:T(8,128)(2,1)S(1)}, bf16[72,896]{1,0:T(8,128)(2,1)S(1)}, u32[]{:S(2)}, u32[]{:S(2)}) collective-permute-start(bf16[72,896]{1,0:T(8,128)(2,1)S(1)} %shard_map.86), channel_id=1, source_target_pairs={{0,16},{16,0},{1,17},{17,1},{2,18},{18,2},{3,19},{19,3},{4,20},{20... | collective-permute-start | bytes 387080 | tf_op jit(solution)/shard_map/ppermute | solution.py:388
  256.2 6.2 %collective-permute-start.5 = (bf16[72,896]{1,0:T(8,128)(2,1)S(1)}, bf16[72,896]{1,0:T(8,128)(2,1)S(1)}, u32[]{:S(2)}, u32[]{:S(2)}) collective-permute-start(bf16[72,896]{1,0:T(8,128)(2,1)S(1)} %add_convert_fusion.refs_0_), channel_id=1, source_target_pairs={{0,96},{32,64},{64,32},{96,0},{1,97},{33,65},{65,33},{97,1},{2,98}... | collective-permute-start | bytes 387080 | tf_op jit(solution)/shard_map/ppermute | solution.py:481
  258.2 6.5 %collective-permute-start.4 = (bf16[72,896]{1,0:T(8,128)(2,1)S(1)}, bf16[72,896]{1,0:T(8,128)(2,1)S(1)}, u32[]{:S(2)}, u32[]{:S(2)}) collective-permute-start(bf16[72,896]{1,0:T(8,128)(2,1)S(1)} %add_convert_fusion.refs_0_), channel_id=1, source_target_pairs={{0,64},{32,96},{64,0},{96,32},{1,65},{33,97},{65,1},{97,33},{2,66}... | collective-permute-start | bytes 387080 | tf_op jit(solution)/shard_map/ppermute | solution.py:481
  258.5 6.2 %collective-permute-start.3 = (bf16[72,896]{1,0:T(8,128)(2,1)S(1)}, bf16[72,896]{1,0:T(8,128)(2,1)S(1)}, u32[]{:S(2)}, u32[]{:S(2)}) collective-permute-start(bf16[72,896]{1,0:T(8,128)(2,1)S(1)} %add_convert_fusion.refs_0_), channel_id=1, source_target_pairs={{0,32},{32,0},{64,96},{96,64},{1,33},{33,1},{65,97},{97,65},{2,34}... | collective-permute-start | bytes 387080 | tf_op jit(solution)/shard_map/ppermute | solution.py:481
Sparse Core Ops, SparseCore 0:
  178.5 48.5 reduce-scatter.1
